TPU v7x, 32 devices: a whole 2x2x4 slice. The times are simulated.
32 devices in a mesh: section: 4 (over z), tp: 8 (over y, x, core).
Axes of the slice: x: 2, y: 2, z: 4, core: 2. Of those that a mesh axis runs over, the one named last changes fastest.
Arguments:
- teacher_rows: bfloat16 [4, 256, 8192], P('section', 'tp'), may hold values from -72 to 72
- norm_gain: float32 [4, 8192], P('section'), may hold values from 0.1 to 1.9
- query_weight: bfloat16 [4, 8192, 8192], P('section', None, 'tp'), may hold values from -2.762136 to 2.762136
- keys_values: bfloat16 [4, 2, 8192, 1024], P('section', None, None, 'tp'), may hold values from -0.071815532 to 0.071815532
- output_weight: bfloat16 [4, 8192, 8192], P('section', 'tp'), may hold values from -0.5 to 0.5
- doc_start: int32 [4], P('section'), may hold values from 1 to 255
- student_rows: bfloat16 [4, 256, 4096], P('section', 'tp'), may hold values from -30 to 30
- projector: bfloat16 [4096, 8192], P('tp', 'section'), may hold values from -1 to 2
Outputs:
- teacher_next: bfloat16 [4, 256, 8192], P('section', 'tp')
- distill_loss: float32 [], replicated
- grad_student: float32 [4, 256, 4096], P('section', 'tp')
- grad_projector: float32 [4096, 8192], P('tp', 'section')
All inputs are finite; a program needn't handle non-finite values.
Results may differ from a plain program's by a relative error of at most 0.02.
Values may be sent and summed in bfloat16 or wider, within the bound.
A program may use at most 128 MiB of HBM per device.

v0:
```python
import math

import jax
import jax.numpy as jnp
from jax import lax
from jax.sharding import PartitionSpec as P

KVH = 8
HD = 128


LOSS_WEIGHT = 64.0
NORM_EPS = 1e-05
COS_EPS = 1e-06


def as_sent(value):
    return jax.tree.map(lambda a: a.astype(jnp.bfloat16) if a.dtype == jnp.float32 else a, value)


def partner(value, axis, apart):
    mask = 2**apart
    pairs = [(source, source ^ mask) for source in range(lax.axis_size(axis))]
    return lax.ppermute(value, axis, pairs)


def round_bf16(values):
    return lax.optimization_barrier(values.astype(jnp.bfloat16)).astype(jnp.float32)


def join_halves(mine, other, low_side):
    return jnp.where(
        low_side, jnp.concatenate([mine, other], axis=1), jnp.concatenate([other, mine], axis=1)
    )


def cosine_step(inner, own_sq, target_sq, student_proj, target):
    inv_own = lax.rsqrt(own_sq + COS_EPS)
    inv_target = lax.rsqrt(target_sq + COS_EPS)
    cosine = inner * inv_own * inv_target
    slope = LOSS_WEIGHT * (
        (inner * inv_target * inv_own * inv_own * inv_own)[:, None] * student_proj
        - target * (inv_own * inv_target)[:, None]
    )
    return (cosine, slope.astype(jnp.bfloat16))


def attend(queries, keys_full, values_full, first_new):
    row_total = queries.shape[0]
    kv_heads = keys_full.shape[1] // HD
    group = queries.shape[1] // HD // kv_heads
    query_heads = queries.reshape(row_total, kv_heads, group, HD)
    key_heads = keys_full.reshape(row_total, kv_heads, HD)
    value_heads = values_full.reshape(row_total, kv_heads, HD)
    scale = 1.0 / math.sqrt(HD)
    scores = (
        jnp.einsum("qegd,ked->egqk", query_heads, key_heads, preferred_element_type=jnp.float32)
        * scale
    )
    positions = jnp.arange(row_total, dtype=jnp.int32)
    after_start = positions >= first_new
    visible = (positions[None, :] <= positions[:, None]) & (
        after_start[None, :] == after_start[:, None]
    )
    scores = jnp.where(visible, scores, -1e30)
    row_max = jnp.max(scores, axis=-1, keepdims=True)
    expo = jnp.where(visible, jnp.exp(scores - row_max), 0.0)
    weights = (expo / jnp.sum(expo, axis=-1, keepdims=True)).astype(jnp.bfloat16)
    mixed = jnp.einsum("egqk,ked->qegd", weights, value_heads, preferred_element_type=jnp.float32)
    return mixed.astype(jnp.bfloat16).reshape(row_total, queries.shape[1])


def shards(
    teacher_rows,
    norm_gain,
    query_weight,
    keys_values,
    output_weight,
    doc_start,
    student_rows,
    projector,
):
    span_rows = teacher_rows[0]
    tp_count = lax.axis_size("tp")
    tp_position = lax.axis_index("tp")
    rows_float = span_rows.astype(jnp.float32)
    mean_square = jnp.mean(rows_float * rows_float, axis=1, keepdims=True)
    normed = (rows_float * lax.rsqrt(mean_square + NORM_EPS) * norm_gain[0][None, :]).astype(
        jnp.bfloat16
    )
    query_local = query_weight[0]
    key_local = keys_values[0, 0]
    value_local = keys_values[0, 1]
    share_count = max(1, tp_count // KVH)
    bit_total = share_count.bit_length() - 1
    query_cols = query_local.shape[1]
    key_cols = key_local.shape[1]
    block_rows = lax.all_gather(normed, "tp", axis=0, tiled=True)
    query_part = jnp.dot(block_rows, query_local, preferred_element_type=jnp.float32).astype(
        jnp.bfloat16
    )
    key_part = jnp.dot(block_rows, key_local, preferred_element_type=jnp.float32).astype(
        jnp.bfloat16
    )
    value_part = jnp.dot(block_rows, value_local, preferred_element_type=jnp.float32).astype(
        jnp.bfloat16
    )
    projected = jnp.concatenate([query_part, key_part, value_part], axis=1)
    queries = projected[:, :query_cols]
    keys_full = projected[:, query_cols : query_cols + key_cols]
    values_full = projected[:, query_cols + key_cols :]
    for bit_index in range(bit_total):
        other_key, other_value = (
            partner(as_sent(keys_full), "tp", bit_index).astype(keys_full.dtype),
            partner(as_sent(values_full), "tp", bit_index).astype(values_full.dtype),
        )
        low_side = tp_position // 2**bit_index % 2 == 0
        keys_full = join_halves(keys_full, other_key, low_side)
        values_full = join_halves(values_full, other_value, low_side)
    mixed_heads = attend(queries, keys_full, values_full, doc_start[0])
    out_local = output_weight[0]
    block = mixed_heads
    attn_sum = lax.psum_scatter(
        round_bf16(jnp.dot(block, out_local, preferred_element_type=jnp.float32)).astype(
            jnp.bfloat16
        ),
        "tp",
        scatter_dimension=0,
        tiled=True,
    ).astype(jnp.float32)
    teacher_next = (rows_float + attn_sum).astype(jnp.bfloat16)
    contract_last = (((1,), (1,)), ((), ()))
    contract_pair = (((0, 1), (0, 1)), ((), ()))
    gathered = lax.all_gather(student_rows, "section", axis=0, tiled=True)
    token_count = gathered.shape[0] * gathered.shape[1]
    token_rows = gathered.reshape(token_count, gathered.shape[2])
    arrived = lax.all_to_all(teacher_next[None], "section", split_axis=2, concat_axis=0, tiled=True)
    target = arrived.reshape(token_count, arrived.shape[2]).astype(jnp.float32)
    student_proj = jnp.dot(
        token_rows,
        lax.all_gather(projector, "tp", axis=0, tiled=True),
        preferred_element_type=jnp.float32,
    )
    inner, own_sq, target_sq = lax.psum(
        (
            jnp.sum(student_proj * target, axis=1),
            jnp.sum(student_proj * student_proj, axis=1),
            jnp.sum(target * target, axis=1),
        ),
        "section",
    )
    cosine, slope = cosine_step(inner, own_sq, target_sq, student_proj, target)
    loss_total = lax.psum(jnp.sum(1.0 - cosine), "tp")
    distill_loss = loss_total / (token_count * tp_count)
    row_terms = lax.dot_general(
        slope,
        lax.all_gather(projector, "tp", axis=0, tiled=True),
        contract_last,
        preferred_element_type=jnp.float32,
    )
    grad_local = lax.psum_scatter(
        row_terms.astype(jnp.bfloat16), "section", scatter_dimension=0, tiled=True
    ).astype(jnp.float32)
    by_column = lax.all_to_all(gathered, "tp", split_axis=2, concat_axis=1, tiled=True)
    slope_stacked = slope.reshape(gathered.shape[0], gathered.shape[1], slope.shape[1])
    block = by_column
    grad_proj = lax.dot_general(
        block,
        lax.all_gather(slope_stacked, "tp", axis=1, tiled=True),
        contract_pair,
        preferred_element_type=jnp.float32,
    )
    return (teacher_next[None], distill_loss, grad_local[None], grad_proj)


def solution(mesh):
    placed = (
        P("section", "tp", None),
        P("section", None),
        P("section", None, "tp"),
        P("section", None, None, "tp"),
        P("section", "tp", None),
        P("section"),
        P("section", "tp", None),
        P("tp", "section"),
    )
    return jax.shard_map(
        shards,
        mesh=mesh,
        in_specs=placed,
        out_specs=(P("section", "tp", None), P(), P("section", "tp", None), P("tp", "section")),
        check_vma=False,
    )
```

profile of v0, /device:TPU:0, one launch (start us, length us, event | category | flops | bytes accessed | tf_op | source)
XLA Modules:
  0.0 369.2 jit_solution(1033365800638313616)
XLA Ops:
  8.0 0.0 all-gather.5.cloned.1.call-start
  8.0 1.3 fusion.38
  9.3 2.0 fusion.40
  11.4 0.0 reduce-scatter.3.cloned.1.call-start
  12.1 0.1 fusion.55
  12.2 38.7 %all-gather.5.cloned.1.call-done = bf16[256,8192]{1,0:T(8,128)(2,1)} async-done(((bf16[32,8192]{1,0:T(8,128)(2,1)}), bf16[256,8192]{1,0:T(8,128)(2,1)}) %all-gather.5.cloned.1.call-update) | async-done | bytes 4194320 | tf_op jit(solution)/shard_map/all_gather | solution.py:98
  50.9 11.5 %fusion.18 = bf16[32,8,8,128]{3,2,1,0:T(8,128)(2,1)S(1)} fusion(bf16[256,8192]{1,0:T(8,128)(2,1)} %all-gather.5.cloned.1.call-done, bf16[1,8192,1024]{2,1,0:T(8,128)(2,1)} %param.10), kind=kOutput, calls=%fused_computation.23 | convolution fusion | flops 4295229440 | bytes 21495808 | tf_op jit(solution)/shard_map/dot_general | solution.py:99
  62.5 4.5 %fusion.13 = (f32[8,256]{1,0:T(8,128)S(1)}, f32[256,256,8]{1,0,2:T(8,128)S(1)}) fusion(pred[256,256]{0,1:T(8,128)(4,1)S(1)} %fusion.55, bf16[32,8,8,128]{3,2,1,0:T(8,128)(2,1)S(1)} %fusion.18, bf16[256,8192]{1,0:T(8,128)(2,1)} %all-gather.5.cloned.1.call-done, bf16[1,2,8192,128]{3,2,1,0:T(8,128)(2,1)} %param.11), kind=kOutput, calls=%fused_computation.16 | convolution fusion | flops 672692224 | bytes 8986624 | tf_op jit(solution)/shard_map/qegd,ked->egqk/dot_general | solution.py:57
  67.0 0.5 fusion.14
  67.5 5.1 %convolution_convert_fusion.1 = bf16[128,8,256]{2,0,1:T(8,128)(2,1)S(1)} fusion(bf16[256,8192]{1,0:T(8,128)(2,1)} %all-gather.5.cloned.1.call-done, bf16[1,2,8192,128]{3,2,1,0:T(8,128)(2,1)} %param.11, f32[256,256,8]{1,0,2:T(8,128)S(1)} %get-tuple-element.21, f32[8,256]{1,0:T(8,128)S(1)} %fusion.14, f32[8,256]{1,0:T(8,128)S(1)} %get-tuple-element.20, ...), kind=kOutput, calls=%fused_computation.21 | convolution fusion | flops 674529280 | bytes 8994816 | tf_op jit(solution)/shard_map/egqk,ked->qegd/dot_general | solution.py:69
  72.6 12.1 %fusion.4 = bf16[256,8192]{1,0:T(8,128)(2,1)} fusion(bf16[256,1024]{0,1:T(8,128)(2,1)S(1)} %bitcast.135, bf16[1,1024,8192]{2,1,0:T(8,128)(2,1)} %param.12), kind=kOutput, calls=%fused_computation.4 | convolution fusion | flops 4297064448 | bytes 21495808 | tf_op jit(solution)/shard_map/dot_general | solution.py:124
  84.7 0.0 all-gather.7.cloned.1.call-start
  84.8 0.5 all-gather.7.cloned.1.call-update
  85.3 0.0 all-gather.9.cloned.1.call-start
  85.4 0.5 all-gather.9.cloned.1.call-update
  85.9 0.2 reduce-scatter.5.cloned.1.call-start
  86.1 71.4 %reduce-scatter.3.cloned.1.call-done = bf16[32,8192]{1,0:T(8,128)(2,1)} async-done(((bf16[256,8192]{1,0:T(8,128)(2,1)}), bf16[32,8192]{1,0:T(8,128)(2,1)}) %reduce-scatter.3.cloned.1.call-update) | async-done | bytes 524304 | tf_op jit(solution)/shard_map/reduce_scatter | solution.py:123
  157.5 1.3 fusion.52
  158.8 6.7 %copy.19 = bf16[1,32,8192]{1,0,2:T(2,128)(2,1)} copy(bf16[1,32,8192]{2,1,0:T(8,128)(2,1)S(1)} %fusion.52) | data formatting | bytes 1048576 | tf_op jit(solution)/shard_map/broadcast_in_dim | solution.py:173
  165.5 0.5 broadcast.47
  166.0 45.2 %reduce.6 = bf16[8192,32]{1,0:T(8,128)(2,1)S(1)} reduce(bf16[8192,1,32]{2,1,0:T(2,128)(2,1)} %bitcast.129, bf16[]{:T(256)} %broadcast.47), dimensions={1}, to_apply=%bitcast.104.reduce_sub_computation | reduce | bytes 1048578
  211.3 2.2 reshape.90
  213.4 18.8 %all_to_all.27 = bf16[4,2,32768]{2,1,0:T(2,128)(2,1)S(1)} all-to-all(bf16[4,2,32768]{2,1,0:T(2,128)(2,1)S(1)} %reshape.90), channel_id=1, replica_groups=mesh['section'=4,'tp'=8] {'section'}, dimensions={0} | all-to-all | bytes 1048576 | tf_op jit(solution)/shard_map/all_to_all | solution.py:137
  232.2 3.3 reshape.91
  235.5 8.4 %bitcast_convert_fusion.1 = f32[1,32,8192]{1,0,2:T(1,128)} fusion(bf16[8192,1,32]{2,1,0:T(2,128)(2,1)} %reshape.91), kind=kLoop, calls=%fused_computation.63 | loop fusion | flops 262144 | bytes 1572864 | tf_op jit(solution)/shard_map/convert_element_type | solution.py:138
  243.9 2.8 copy.20
  246.7 8.4 %convert_multiply_fusion.2 = f32[1,32,8192]{1,0,2:T(1,128)} fusion(bf16[8192,1,32]{2,1,0:T(2,128)(2,1)} %reshape.91), kind=kLoop, calls=%fused_computation.58 | loop fusion | flops 524288 | bytes 1572864 | tf_op jit(solution)/shard_map/mul | solution.py:148
  255.2 2.5 reduce_sum.62
  257.6 0.1 copy.27
  257.7 0.1 copy.22
  257.8 0.1 reduce_sum.64
  257.9 8.6 %multiply_reduce_fusion = (f32[128]{0:T(128)S(1)}, f32[128]{0:T(128)S(1)}, f32[128,2048]{1,0:T(8,128)S(1)}) fusion(f32[1,32,4,2048]{3,1,2,0:T(8,128)S(1)} %copy.20, bf16[128,4096]{1,0:T(8,128)(2,1)} %bitcast.132, bf16[4096,2048]{1,0:T(8,128)(2,1)} %all-gather.9.cloned.1.call-done), kind=kOutput, calls=%fused_computation.40 | convolution fusion | flops 2148532224 | bytes 19923968 | tf_op jit(solution)/shard_map/dot_general | solution.py:139
  266.5 10.0 %all-reduce = (f32[128]{0:T(128)S(1)}, f32[128]{0:T(128)S(1)}, f32[128]{0:T(128)S(1)}) all-reduce(f32[128]{0:T(128)S(1)} %get-tuple-element.13, f32[128]{0:T(128)S(1)} %get-tuple-element.12, f32[128]{0:T(128)S(1)} %reduce_sum.64), channel_id=1, replica_groups=mesh['section'=4,'tp'=8] {'section'}, use_global_device_ids=true, to_apply=%region_5.6 | all-reduce | flops 384 | bytes 3072 | tf_op jit(solution)/shard_map/psum | solution.py:144
  276.6 0.6 multiply_multiply_fusion
  277.2 0.2 fusion.45
  277.4 12.6 %convolution_convert_fusion = bf16[128,4096]{1,0:T(8,128)(2,1)} fusion(bf16[128,2048]{1,0:T(8,128)(2,1)S(1)} %fusion.45, bf16[4096,2048]{1,0:T(8,128)(2,1)} %all-gather.9.cloned.1.call-done), kind=kOutput, calls=%fused_computation.5 | convolution fusion | flops 2148007936 | bytes 18350080 | tf_op jit(solution)/shard_map/dot_general | solution.py:155
  290.0 0.0 all-gather.11.cloned.1.call-start
  290.1 0.7 all-gather.11.cloned.1.call-update
  290.8 4.6 %copy.23 = bf16[4,32,4096]{1,0,2:T(4,128)(2,1)} copy(bf16[4,32,4096]{2,1,0:T(8,128)(2,1)S(1)} %copy-done) | data formatting | bytes 2097152 | tf_op jit(solution)/shard_map/all_gather | solution.py:134
  295.4 7.0 %reshape.92 = bf16[8,2,32768]{2,1,0:T(2,128)(2,1)S(1)} reshape(bf16[4096,4,32]{2,1,0:T(4,128)(2,1)} %bitcast.127) | data formatting | bytes 2097152
  302.5 21.5 %all_to_all.28 = bf16[8,2,32768]{2,1,0:T(2,128)(2,1)S(1)} all-to-all(bf16[8,2,32768]{2,1,0:T(2,128)(2,1)S(1)} %reshape.92), channel_id=1, replica_groups=mesh['section'=4,'tp'=8] {'tp'}, dimensions={0} | all-to-all | bytes 2097152 | tf_op jit(solution)/shard_map/all_to_all | solution.py:164
  324.0 4.5 %reshape.93 = bf16[4096,4,32]{2,1,0:T(4,128)(2,1)} reshape(bf16[8,2,32768]{2,1,0:T(2,128)(2,1)S(1)} %all_to_all.28) | data formatting | bytes 2097152
  328.5 5.5 %copy.24 = bf16[4,32,8,512]{3,1,2,0:T(8,128)(2,1)S(1)} copy(bf16[4,32,8,512]{1,0,3,2:T(4,128)(2,1)} %bitcast.128) | data formatting | bytes 2097152 | tf_op jit(solution)/shard_map/all_to_all | solution.py:164
  334.0 12.4 %psum.31 = f32[]{:T(128)} all-reduce(f32[]{:T(128)} %get-tuple-element.18), channel_id=1, replica_groups=mesh['section'=4,'tp'=8] {'tp'}, use_global_device_ids=true, to_apply=%region_11.12 | all-reduce | flops 1 | bytes 8 | tf_op jit(solution)/shard_map/psum | solution.py:153
  347.1 0.0 reduce-scatter.5.cloned.1.call-done
  347.1 1.8 bitcast_convert_fusion
  348.9 6.5 %convolution_bitcast_fusion = f32[512,2048]{0,1:T(8,128)} fusion(bf16[4,256,2048]{2,1,0:T(8,128)(2,1)} %all-gather.11.cloned.1.call-done, bf16[4,256,512]{2,1,0:T(8,128)(2,1)S(1)} %bitcast.134), kind=kOutput, calls=%fused_computation.6 | convolution fusion | flops 2147483648 | bytes 9437184 | tf_op jit(solution)/shard_map/dot_general | solution.py:167
  355.4 5.3 %copy.25 = f32[512,2048]{1,0:T(8,128)} copy(f32[512,2048]{0,1:T(8,128)} %convolution_bitcast_fusion) | data formatting | bytes 8388608
  (16 shorter events, 0.1 us)
Async XLA Ops:
  8.0 42.9 %all-gather.5.cloned.1.call-start = ((), (), s32[]{:S(2)}) async-start(), calls=%async_computation.4 | async-start | bytes 4718592 | tf_op jit(solution)/shard_map/all_gather | solution.py:98
  11.4 146.1 %reduce-scatter.3.cloned.1.call-start = ((), (), s32[]{:S(2)}) async-start(), calls=%async_computation.5 | async-start | bytes 4718592 | tf_op jit(solution)/shard_map/reduce_scatter | solution.py:123
  84.7 72.8 %copy-start.2 = (bf16[1,32,8192]{2,1,0:T(8,128)(2,1)S(1)}, bf16[1,32,8192]{2,1,0:T(8,128)(2,1)}, u32[]{:S(2)}) copy-start(bf16[1,32,8192]{2,1,0:T(8,128)(2,1)} %param.8) | copy-start | bytes 1572868
  84.7 173.1 %all-gather.7.cloned.1.call-start = ((), (), s32[]{:S(2)}) async-start(), calls=%async_computation.6 | async-start | bytes 1310720 | tf_op jit(solution)/shard_map/all_gather | solution.py:134
  85.3 172.6 %all-gather.9.cloned.1.call-start = ((), (), s32[]{:S(2)}) async-start(), calls=%async_computation.7 | async-start | bytes 18874368 | tf_op jit(solution)/shard_map/all_gather | solution.py:141
  85.9 261.2 %reduce-scatter.5.cloned.1.call-start = ((), (), s32[]{:S(2)}) async-start(), calls=%async_computation.8 | async-start | bytes 1310720 | tf_op jit(solution)/shard_map/reduce_scatter | solution.py:161
  158.8 52.4 %copy-start.3 = (bf16[1,32,8192]{2,1,0:T(8,128)(2,1)}, bf16[1,32,8192]{2,1,0:T(8,128)(2,1)S(1)}, u32[]{:S(2)}) copy-start(bf16[1,32,8192]{2,1,0:T(8,128)(2,1)S(1)} %fusion.52) | copy-start | bytes 1572868
  277.4 12.6 %copy-start.1 = (bf16[128,2048]{1,0:T(8,128)(2,1)}, bf16[128,2048]{1,0:T(8,128)(2,1)S(1)}, u32[]{:S(2)}) copy-start(bf16[128,2048]{1,0:T(8,128)(2,1)S(1)} %fusion.45) | copy-start | bytes 1572868
  277.4 13.4 %copy-start = (bf16[4,32,4096]{2,1,0:T(8,128)(2,1)S(1)}, bf16[4,32,4096]{2,1,0:T(8,128)(2,1)}, u32[]{:S(2)}) copy-start(bf16[4,32,4096]{2,1,0:T(8,128)(2,1)} %all-gather.7.cloned.1.call-done) | copy-start | bytes 3145732
  290.0 58.8 %all-gather.11.cloned.1.call-start = ((), (), s32[]{:S(2)}) async-start(), calls=%async_computation.9 | async-start | bytes 4718592 | tf_op jit(solution)/shard_map/all_gather | solution.py:169
Sparse Core Ops, SparseCore 0:
  11.5 39.4 all-gather.4
  84.9 72.5 reduce-scatter.2
  292.8 39.5 all-gather.10
Sparse Core Ops, SparseCore 1:
  86.9 27.8 all-gather.6
  116.7 89.4 all-gather.8
  290.1 24.3 reduce-scatter.4
where the time goes:
time: 370 us; the launch traced here: 369 us
  waiting for transfers between devices  112 us (30%)
  other arithmetic  72.4 us (20%)
  blocking collectives  62.8 us (17%)
  matrix products  61 us (16%)
  local copies, waits for them, and re-layouts  42.7 us (12%)
  between operations  18 us (5%)
    reduce_scatter x1, waiting for transfers between devices, shards(): lax.psum_scatter(round_bf16(jnp.dot(block, out_local, preferred_element_t...  71.4 us
    unnamed x1, other arithmetic  45.2 us
    all_gather x1, waiting for transfers between devices, shards(): block_rows = lax.all_gather(normed, 'tp', axis=0, tiled=True)  38.7 us
    unnamed x15, local copies, waits for them, and re-layouts  22.9 us
    all_to_all x1, blocking collectives, shards(): lax.all_to_all(gathered, 'tp', split_axis=2, concat_axis=1, tiled=True)  21.5 us
    all_to_all x1, blocking collectives, shards(): lax.all_to_all(teacher_next[None], 'section', split_axis=2, concat_axis=0...  18.8 us
    dot_general x1, matrix products, shards(): lax.dot_general(slope, lax.all_gather(projector, 'tp', axis=0, tiled=True...  12.6 us
    psum x1, blocking collectives, shards(): loss_total = lax.psum(jnp.sum(1.0 - cosine), 'tp')  12.4 us
  transfers between devices with their start and end apart: 6, of which 2 were waited for; matrix products, arithmetic and copies ran while one was open for 28% of the time, Pallas kernels for 0%

commit v1 on v0

--- a/solution.py
+++ b/solution.py
@@ -1,8 +1,11 @@
+import functools
 import math
 
 import jax
 import jax.numpy as jnp
 from jax import lax
+from jax.experimental import pallas as pl
+from jax.experimental.pallas import tpu as pltpu
 from jax.sharding import PartitionSpec as P
 
 KVH = 8
@@ -173,7 +176,684 @@
     return (teacher_next[None], distill_loss, grad_local[None], grad_proj)
 
 
+MESH = pl.DeviceIdType.MESH
+F32 = jnp.float32
+BF16 = jnp.bfloat16
+SECTIONS = 4
+TPS = 8
+VMEM_LIMIT = 58 * 1024 * 1024
+
+
+def places():
+    section = lax.axis_index("section")
+    tp = lax.axis_index("tp")
+    core = tp % 2
+    x = (tp // 2) % 2
+    y = tp // 4
+    sib = tp + 1 - 2 * core
+    xn = tp + 2 - 4 * x
+    yn = tp + 4 - 8 * y
+    first = (1 - core) * xn + core * yn
+    second = core * xn + (1 - core) * yn
+    diag = xn + 4 - 8 * y
+    return section, tp, core, x, y, sib, first, second, diag
+
+
+def greet_all(section, tp):
+    barrier = pltpu.get_barrier_semaphore()
+    me = section * TPS + tp
+
+    def one(step, carry):
+        other = (me + step) % (SECTIONS * TPS)
+        pl.semaphore_signal(
+            barrier, inc=1, device_id=(other // TPS, other % TPS), device_id_type=MESH
+        )
+        return carry
+
+    lax.fori_loop(1, SECTIONS * TPS, one, 0)
+    pl.semaphore_wait(barrier, SECTIONS * TPS - 1)
+
+
+def greet(peers):
+    barrier = pltpu.get_barrier_semaphore()
+    for peer in peers:
+        pl.semaphore_signal(barrier, inc=1, device_id=peer, device_id_type=MESH)
+    pl.semaphore_wait(barrier, len(peers))
+
+
+def gather_ops(buf, rows, send_sem, recv_sem):
+    section, tp, core, x, y, sib, first, second, diag = places()
+
+    def copy(kind, chunk, owner, target):
+        place = buf.at[chunk, pl.ds(pl.multiple_of(owner * rows, rows), rows)]
+        return pltpu.make_async_remote_copy(
+            src_ref=place,
+            dst_ref=place,
+            send_sem=send_sem.at[kind, chunk],
+            recv_sem=recv_sem.at[kind, chunk],
+            device_id=(section, target),
+            device_id_type=MESH,
+        )
+
+    def begin(chunk):
+        copy(0, chunk, tp, first).start()
+        copy(1, chunk, tp, second).start()
+        copy(2, chunk, tp, sib).start()
+
+    def forward(chunk):
+        copy(0, chunk, tp, first).wait_recv()
+        copy(3, chunk, first, second).start()
+        copy(4, chunk, first, sib).start()
+        copy(1, chunk, tp, second).wait_recv()
+        copy(5, chunk, second, sib).start()
+
+    def across(chunk):
+        copy(3, chunk, first, second).wait_recv()
+        copy(6, chunk, diag, sib).start()
+
+    def arrive(chunk):
+        copy(2, chunk, tp, sib).wait_recv()
+        copy(4, chunk, first, sib).wait_recv()
+        copy(5, chunk, second, sib).wait_recv()
+        copy(6, chunk, diag, sib).wait_recv()
+
+    def drain(chunk):
+        for kind in range(7):
+            copy(kind, chunk, tp, sib).wait_send()
+
+    return begin, forward, across, arrive, drain
+
+
+def project_kernel(
+    normed, student, wq_hbm, wkv_hbm,
+    qkv, feats,
+    buf, wq, wkv, acc, acc_k, acc_v,
+    g_send, g_recv, s_send, s_recv, w_sem,
+):
+    section, tp, core, x, y, sib, first, second, diag = places()
+    chunks, width = buf.shape[0], buf.shape[2]
+    rows = normed.shape[0]
+    part = feats.shape[3]
+    me = section * TPS + tp
+
+    def wq_copy(c):
+        at = pl.ds(pl.multiple_of(c * width, width), width)
+        return pltpu.make_async_copy(wq_hbm.at[at], wq.at[at], w_sem.at[0, c])
+
+    def wkv_copy(c):
+        at = pl.ds(pl.multiple_of(c * width, width), width)
+        return pltpu.make_async_copy(wkv_hbm.at[:, at], wkv.at[:, at], w_sem.at[1, c])
+
+    def load(c, carry):
+        wq_copy(c).start()
+        wkv_copy(c).start()
+        at = pl.ds(pl.multiple_of(c * width, width), width)
+        buf[c, pl.ds(pl.multiple_of(tp * rows, rows), rows)] = normed[:, at]
+        return carry
+
+    lax.fori_loop(0, chunks, load, 0)
+    feats[tp, section] = student[:, pl.ds(pl.multiple_of(tp * part, part), part)]
+    acc[...] = jnp.zeros_like(acc)
+    acc_k[...] = jnp.zeros_like(acc_k)
+    acc_v[...] = jnp.zeros_like(acc_v)
+    greet_all(section, tp)
+    begin, forward, across, arrive, drain = gather_ops(buf, rows, g_send, g_recv)
+
+    def s_copy(step):
+        other = (me + step) % (SECTIONS * TPS)
+        to_section, to_tp = other // TPS, other % TPS
+        return pltpu.make_async_remote_copy(
+            src_ref=student.at[:, pl.ds(pl.multiple_of(to_tp * part, part), part)],
+            dst_ref=feats.at[tp, section],
+            send_sem=s_send.at[step],
+            recv_sem=s_recv.at[step],
+            device_id=(to_section, to_tp),
+            device_id_type=MESH,
+        )
+
+    def start_gather(c, carry):
+        begin(c)
+        return carry
+
+    lax.fori_loop(0, chunks, start_gather, 0)
+
+    def start_student(step, carry):
+        s_copy(step).start()
+        return carry
+
+    lax.fori_loop(1, SECTIONS * TPS, start_student, 0)
+
+    def step(i, carry):
+        @pl.when(i < chunks)
+        def _():
+            forward(i)
+
+        @pl.when((i >= 1) & (i < chunks + 1))
+        def _():
+            across(i - 1)
+
+        @pl.when(i >= 2)
+        def _():
+            c = i - 2
+            arrive(c)
+            wq_copy(c).wait()
+            wkv_copy(c).wait()
+            at = pl.ds(pl.multiple_of(c * width, width), width)
+            block = buf[c]
+            acc[...] += jnp.dot(block, wq[at], preferred_element_type=F32)
+            acc_k[...] += jnp.dot(block, wkv[0, at], preferred_element_type=F32)
+            acc_v[...] += jnp.dot(block, wkv[1, at], preferred_element_type=F32)
+
+        return carry
+
+    lax.fori_loop(0, chunks + 2, step, 0)
+    q_cols = acc.shape[1]
+    k_cols = acc_k.shape[1]
+    qkv[:, :q_cols] = acc[...].astype(BF16)
+    qkv[:, q_cols : q_cols + k_cols] = acc_k[...].astype(BF16)
+    qkv[:, q_cols + k_cols :] = acc_v[...].astype(BF16)
+
+    def finish(c, carry):
+        drain(c)
+        return carry
+
+    lax.fori_loop(0, chunks, finish, 0)
+
+    def finish_student(step, carry):
+        s_copy(step).wait()
+        return carry
+
+    lax.fori_loop(1, SECTIONS * TPS, finish_student, 0)
+
+
+def project(normed, student, wq, wkv):
+    rows, depth = normed.shape
+    total = rows * TPS
+    q_cols, k_cols = wq.shape[1], wkv.shape[2]
+    chunks = 8
+    part = student.shape[1] // TPS
+    vmem = pl.BlockSpec(memory_space=pltpu.VMEM)
+    hbm = pl.BlockSpec(memory_space=pl.ANY)
+    return pl.pallas_call(
+        project_kernel,
+        out_shape=(
+            jax.ShapeDtypeStruct((total, q_cols + 2 * k_cols), BF16),
+            jax.ShapeDtypeStruct((TPS, SECTIONS, rows, part), BF16),
+        ),
+        in_specs=[vmem, vmem, hbm, hbm],
+        out_specs=(vmem, vmem),
+        scratch_shapes=[
+            pltpu.VMEM((chunks, total, depth // chunks), BF16),
+            pltpu.VMEM(wq.shape, BF16),
+            pltpu.VMEM(wkv.shape, BF16),
+            pltpu.VMEM((total, q_cols), F32),
+            pltpu.VMEM((total, k_cols), F32),
+            pltpu.VMEM((total, k_cols), F32),
+            pltpu.SemaphoreType.DMA((7, chunks)),
+            pltpu.SemaphoreType.DMA((7, chunks)),
+            pltpu.SemaphoreType.DMA((SECTIONS * TPS,)),
+            pltpu.SemaphoreType.DMA((SECTIONS * TPS,)),
+            pltpu.SemaphoreType.DMA((2, chunks)),
+        ],
+        compiler_params=pltpu.CompilerParams(
+            collective_id=0, has_side_effects=True, vmem_limit_bytes=VMEM_LIMIT
+        ),
+        name="gather_project",
+    )(normed, student, wq, wkv)
+
+
+def scatter_kernel(
+    teacher, lhs, rhs_hbm, *refs,
+):
+    if teacher:
+        resid, out, shared = refs[:3]
+        refs = refs[3:]
+    else:
+        out = refs[0]
+        refs = refs[1:]
+    rhs, part, sib_buf, pair, got1, half, got2, sends, recvs, w_sem = refs[:10]
+    if teacher:
+        z_send, z_recv = refs[10:]
+    section, tp, core, x, y, sib, first, second, diag = places()
+    chunks, _, m, width = part.shape
+    f_mine = (1 - core) * x + core * y
+    g_mine = core * x + (1 - core) * y
+
+    def column(i):
+        if teacher:
+            return (i % SECTIONS) * (chunks // SECTIONS) + i // SECTIONS
+        return i
+
+    def columns(i):
+        return pl.ds(pl.multiple_of(column(i) * width, width), width)
+
+    def w_copy(i):
+        return pltpu.make_async_copy(rhs_hbm.at[:, columns(i)], rhs.at[i], w_sem.at[i])
+
+    def load(i, carry):
+        w_copy(i).start()
+        return carry
+
+    lax.fori_loop(0, chunks, load, 0)
+    peers = [(section, sib), (section, first), (section, second)]
+    if teacher:
+        peers += [((section + d) % SECTIONS, tp) for d in range(1, SECTIONS)]
+    greet(peers)
+
+    def remote(kind, i, source, landing, target):
+        return pltpu.make_async_remote_copy(
+            src_ref=source,
+            dst_ref=landing,
+            send_sem=sends.at[kind, i],
+            recv_sem=recvs.at[kind, i],
+            device_id=(section, target),
+            device_id_type=MESH,
+        )
+
+    def to_sib(i):
+        return remote(0, i, part.at[i, pl.ds(4 * (1 - core), 4)], sib_buf.at[i], sib)
+
+    def to_first(i):
+        return remote(1, i, pair.at[i, 1 - f_mine], got1.at[i], first)
+
+    def to_second(i):
+        return remote(2, i, half.at[i, 1 - g_mine], got2.at[i], second)
+
+    def to_z(i, d):
+        return pltpu.make_async_remote_copy(
+            src_ref=out.at[:, columns(i)],
+            dst_ref=shared.at[section, :, pl.ds(pl.multiple_of((i // SECTIONS) * width, width), width)],
+            send_sem=z_send.at[i],
+            recv_sem=z_recv.at[section, i // SECTIONS],
+            device_id=(i % SECTIONS, tp),
+            device_id_type=MESH,
+        )
+
+    def from_z(other, h):
+        place = shared.at[other, :, pl.ds(pl.multiple_of(h * width, width), width)]
+        return pltpu.make_async_remote_copy(
+            src_ref=place,
+            dst_ref=place,
+            send_sem=z_send.at[0],
+            recv_sem=z_recv.at[other, h],
+            device_id=(other, tp),
+            device_id_type=MESH,
+        )
+
+    def stage_a(i):
+        w_copy(i).wait()
+        block = jnp.dot(lhs[...], rhs[i], preferred_element_type=F32).astype(BF16)
+        for t in range(TPS):
+            yy, xx, cc = t // 4, (t // 2) % 2, t % 2
+            slot = 4 * cc + 2 * (yy if cc else xx) + (xx if cc else yy)
+            part[i, slot] = block[t * m : (t + 1) * m]
+        to_sib(i).start()
+
+    def stage_b(i):
+        to_sib(i).wait_recv()
+        for f in range(2):
+            for g in range(2):
+                mine = part[i, 4 * core + 2 * f + g].astype(F32)
+                pair[i, f, g] = (mine + sib_buf[i, 2 * f + g].astype(F32)).astype(BF16)
+        to_first(i).start()
+
+    def stage_c(i):
+        to_first(i).wait_recv()
+        for g in range(2):
+            half[i, g] = (pair[i, f_mine, g].astype(F32) + got1[i, g].astype(F32)).astype(BF16)
+        to_second(i).start()
+
+    def stage_d(i):
+        to_second(i).wait_recv()
+        total = half[i, g_mine].astype(F32) + got2[i].astype(F32)
+        if not teacher:
+            out[:, columns(i)] = total
+            return
+        value = (resid[:, columns(i)].astype(F32) + total).astype(BF16)
+        out[:, columns(i)] = value
+
+        @pl.when(i % SECTIONS == section)
+        def _():
+            at = pl.ds(pl.multiple_of((i // SECTIONS) * width, width), width)
+            shared[section, :, at] = value
+
+        @pl.when(i % SECTIONS != section)
+        def _():
+            to_z(i, 0).start()
+
+    ends = (0, 1, 3, 5)
+
+    def step(i, carry):
+        for late, stage in zip(ends, (stage_a, stage_b, stage_c, stage_d)):
+
+            @pl.when((i >= late) & (i < chunks + late))
+            def _():
+                stage(i - late)
+
+        return carry
+
+    lax.fori_loop(0, chunks + ends[-1], step, 0)
+
+    def finish(i, carry):
+        to_sib(i).wait_send()
+        to_first(i).wait_send()
+        to_second(i).wait_send()
+        if teacher:
+
+            @pl.when(i % SECTIONS != section)
+            def _():
+                to_z(i, 0).wait_send()
+
+            @pl.when(i % SECTIONS != section)
+            def _():
+                from_z(i % SECTIONS, i // SECTIONS).wait_recv()
+
+        return carry
+
+    lax.fori_loop(0, chunks, finish, 0)
+
+
+def scatter(lhs, rhs, resid=None):
+    teacher = resid is not None
+    depth, cols = rhs.shape
+    m = lhs.shape[0] // TPS
+    chunks = 8
+    width = cols // chunks
+    vmem = pl.BlockSpec(memory_space=pltpu.VMEM)
+    hbm = pl.BlockSpec(memory_space=pl.ANY)
+    scratch = [
+        pltpu.VMEM((chunks, depth, width), BF16),
+        pltpu.VMEM((chunks, TPS, m, width), BF16),
+        pltpu.VMEM((chunks, 4, m, width), BF16),
+        pltpu.VMEM((chunks, 2, 2, m, width), BF16),
+        pltpu.VMEM((chunks, 2, m, width), BF16),
+        pltpu.VMEM((chunks, 2, m, width), BF16),
+        pltpu.VMEM((chunks, m, width), BF16),
+        pltpu.SemaphoreType.DMA((3, chunks)),
+        pltpu.SemaphoreType.DMA((3, chunks)),
+        pltpu.SemaphoreType.DMA((chunks,)),
+    ]
+    if teacher:
+        scratch += [
+            pltpu.SemaphoreType.DMA((chunks,)),
+            pltpu.SemaphoreType.DMA((SECTIONS, chunks // SECTIONS)),
+        ]
+        shape = (
+            jax.ShapeDtypeStruct((m, cols), BF16),
+            jax.ShapeDtypeStruct((SECTIONS, m, cols // SECTIONS), BF16),
+        )
+        operands = (lhs, rhs, resid)
+    else:
+        shape = jax.ShapeDtypeStruct((m, cols), F32)
+        operands = (lhs, rhs)
+    return pl.pallas_call(
+        functools.partial(scatter_kernel, teacher),
+        out_shape=shape,
+        in_specs=[vmem, hbm] + [vmem] * (len(operands) - 2),
+        out_specs=jax.tree.map(lambda _: vmem, shape),
+        scratch_shapes=scratch,
+        compiler_params=pltpu.CompilerParams(
+            collective_id=1 if teacher else 2, has_side_effects=True, vmem_limit_bytes=VMEM_LIMIT
+        ),
+        name="scatter_teacher" if teacher else "scatter_student",
+    )(*operands)
+
+
+def grad_kernel(
+    student_proj, target, feats, proj_hbm,
+    grad_s, grad_p, loss,
+    proj, buf, gs, gs_out, landed, sums, sums_in, flat, back,
+    g_send, g_recv, a_send, a_recv, z_send, z_recv, w_sem,
+):
+    section, tp, core, x, y, sib, first, second, diag = places()
+    me = section * TPS + tp
+    chunks, _, width = buf.shape
+    rows = grad_s.shape[0]
+    parts = chunks // SECTIONS
+    load = pltpu.make_async_copy(proj_hbm, proj, w_sem.at[0])
+    load.start()
+    own = student_proj[...]
+    goal = target[...].astype(F32)
+    lane = lax.broadcasted_iota(jnp.int32, (own.shape[0], 128), 1)
+    inner = jnp.sum(own * goal, axis=1, keepdims=True)
+    own_sq = jnp.sum(own * own, axis=1, keepdims=True)
+    goal_sq = jnp.sum(goal * goal, axis=1, keepdims=True)
+    table = jnp.where(lane == 0, inner, jnp.where(lane == 1, own_sq, goal_sq))
+    flat[...] = table.T
+    sums[...] = flat[:8]
+    greet_all(section, tp)
+
+    def a_copy(d):
+        other = (section + d) % SECTIONS
+        return pltpu.make_async_remote_copy(
+            src_ref=sums,
+            dst_ref=sums_in.at[d - 1],
+            send_sem=a_send.at[d - 1],
+            recv_sem=a_recv.at[d - 1],
+            device_id=(other, tp),
+            device_id_type=MESH,
+        )
+
+    for d in (2, 1, 3):
+        a_copy(d).start()
+    grad_p[...] = jnp.zeros_like(grad_p)
+    for d in (1, 2, 3):
+        a_copy(d).wait()
+    flat[:8] = sums[...] + sums_in[0] + sums_in[1] + sums_in[2]
+    back[...] = flat[...].T
+    table = back[...]
+    inner, own_sq, goal_sq = table[:, 0:1], table[:, 1:2], table[:, 2:3]
+    inv_own = lax.rsqrt(own_sq + COS_EPS)
+    inv_goal = lax.rsqrt(goal_sq + COS_EPS)
+    cosine = inner * inv_own * inv_goal
+    loss[...] = jnp.broadcast_to(1.0 - cosine, loss.shape)
+    up = LOSS_WEIGHT * (inner * inv_goal * inv_own * inv_own * inv_own)
+    down = LOSS_WEIGHT * (inv_own * inv_goal)
+    back[...] = jnp.where(lane == 0, up, down)
+
+    def block_of(i):
+        return (section + 2 + i // parts) % SECTIONS, i % parts
+
+    def at_tp(index):
+        return pl.ds(pl.multiple_of(index * rows, rows), rows)
+
+    begin, forward, across, arrive, drain = gather_ops(buf, rows, g_send, g_recv)
+
+    def make(i, carry):
+        s, h = block_of(i)
+        tokens = at_tp(s)
+        cols = pl.ds(pl.multiple_of(h * width, width), width)
+        scale = back[tokens]
+        piece = (
+            scale[:, 0:1] * student_proj[tokens, cols]
+            - scale[:, 1:2] * target[tokens, cols].astype(F32)
+        )
+        buf[i, at_tp(tp)] = piece.astype(BF16)
+        begin(i)
+        return carry
+
+    lax.fori_loop(0, chunks, make, 0)
+    load.wait()
+
+    def z_copy(s, step):
+        other = (tp + step) % TPS
+        return pltpu.make_async_remote_copy(
+            src_ref=gs_out.at[s, at_tp(other)],
+            dst_ref=landed.at[section, tp],
+            send_sem=z_send.at[s, step],
+            recv_sem=z_recv.at[section, tp],
+            device_id=(s, other),
+            device_id_type=MESH,
+        )
+
+    def z_land(s, t):
+        place = landed.at[s, t]
+        return pltpu.make_async_remote_copy(
+            src_ref=place,
+            dst_ref=place,
+            send_sem=z_send.at[0, 0],
+            recv_sem=z_recv.at[s, t],
+            device_id=(section, tp),
+            device_id_type=MESH,
+        )
+
+    last_dims = (((1,), (1,)), ((), ()))
+    first_dims = (((0,), (0,)), ((), ()))
+
+    def use(i):
+        s, h = block_of(i)
+        arrive(i)
+        cols = pl.ds(pl.multiple_of(h * width, width), width)
+        slopes = buf[i]
+        term = lax.dot_general(slopes, proj[:, cols], last_dims, preferred_element_type=F32)
+
+        @pl.when(h == 0)
+        def _():
+            gs[...] = term
+
+        @pl.when(h > 0)
+        def _():
+            gs[...] += term
+
+        @pl.when(h == parts - 1)
+        def _():
+            gs_out[s] = gs[...].astype(BF16)
+
+            def push(step, carry):
+                @pl.when((s != section) | (step > 0))
+                def _():
+                    z_copy(s, step).start()
+
+                return carry
+
+            lax.fori_loop(0, TPS, push, 0)
+
+            @pl.when(s == section)
+            def _():
+                landed[section, tp] = gs_out[section, at_tp(tp)]
+
+        tokens = feats[:, s].reshape(TPS * rows, feats.shape[3])
+        grad_p[:, cols] += lax.dot_general(tokens, slopes, first_dims, preferred_element_type=F32)
+
+    def step(i, carry):
+        @pl.when(i < chunks)
+        def _():
+            forward(i)
+
+        @pl.when((i >= 1) & (i < chunks + 1))
+        def _():
+            across(i - 1)
+
+        @pl.when(i >= 2)
+        def _():
+            use(i - 2)
+
+        return carry
+
+    lax.fori_loop(0, chunks + 2, step, 0)
+
+    def finish(i, carry):
+        drain(i)
+        return carry
+
+    lax.fori_loop(0, chunks, finish, 0)
+
+    def finish_z(i, carry):
+        s, step = i // TPS, i % TPS
+
+        @pl.when((s != section) | (step > 0))
+        def _():
+            z_copy(s, step).wait_send()
+
+        @pl.when((s != section) | (step != tp))
+        def _():
+            z_land(s, step).wait_recv()
+
+        return carry
+
+    lax.fori_loop(0, SECTIONS * TPS, finish_z, 0)
+    part = landed.shape[3]
+    for t in range(TPS):
+        total = landed[0, t].astype(F32)
+        for s in range(1, SECTIONS):
+            total += landed[s, t].astype(F32)
+        grad_s[:, t * part : (t + 1) * part] = total
+
+
+def gradients(student_proj, target, feats, proj):
+    tokens, cols = student_proj.shape
+    rows = tokens // SECTIONS
+    part = feats.shape[3]
+    chunks = 8
+    width = cols * SECTIONS // chunks
+    vmem = pl.BlockSpec(memory_space=pltpu.VMEM)
+    hbm = pl.BlockSpec(memory_space=pl.ANY)
+    dma = pltpu.SemaphoreType.DMA
+    return pl.pallas_call(
+        grad_kernel,
+        out_shape=(
+            jax.ShapeDtypeStruct((rows, part * TPS), F32),
+            jax.ShapeDtypeStruct((part, cols), F32),
+            jax.ShapeDtypeStruct((tokens, 128), F32),
+        ),
+        in_specs=[vmem, vmem, vmem, hbm],
+        out_specs=(vmem, vmem, vmem),
+        scratch_shapes=[
+            pltpu.VMEM(proj.shape, BF16),
+            pltpu.VMEM((chunks, TPS * rows, width), BF16),
+            pltpu.VMEM((TPS * rows, part), F32),
+            pltpu.VMEM((SECTIONS, TPS * rows, part), BF16),
+            pltpu.VMEM((SECTIONS, TPS, rows, part), BF16),
+            pltpu.VMEM((8, tokens), F32),
+            pltpu.VMEM((SECTIONS - 1, 8, tokens), F32),
+            pltpu.VMEM((128, tokens), F32),
+            pltpu.VMEM((tokens, 128), F32),
+            dma((7, chunks)),
+            dma((7, chunks)),
+            dma((SECTIONS - 1,)),
+            dma((SECTIONS - 1,)),
+            dma((SECTIONS, TPS)),
+            dma((SECTIONS, TPS)),
+            dma((1,)),
+        ],
+        compiler_params=pltpu.CompilerParams(
+            collective_id=3, has_side_effects=True, vmem_limit_bytes=VMEM_LIMIT
+        ),
+        name="slope_gradients",
+    )(student_proj, target, feats, proj)
+
+
+def kernel_shards(
+    teacher_rows,
+    norm_gain,
+    query_weight,
+    keys_values,
+    output_weight,
+    doc_start,
+    student_rows,
+    projector,
+):
+    span_rows = teacher_rows[0]
+    rows_float = span_rows.astype(F32)
+    mean_square = jnp.mean(rows_float * rows_float, axis=1, keepdims=True)
+    normed = (rows_float * lax.rsqrt(mean_square + NORM_EPS) * norm_gain[0][None, :]).astype(BF16)
+    qkv, feats = project(normed, student_rows[0], query_weight[0], keys_values[0])
+    q_cols = query_weight.shape[2]
+    student_proj = scatter(feats.reshape(-1, feats.shape[3]), projector)
+    mixed = attend(
+        qkv[:, :q_cols], qkv[:, q_cols : q_cols + HD], qkv[:, q_cols + HD :], doc_start[0]
+    )
+    teacher_next, target = scatter(mixed, output_weight[0], span_rows)
+    grad_local, grad_proj, loss_rows = gradients(
+        student_proj, target.reshape(-1, target.shape[2]), feats, projector
+    )
+    loss_total = lax.psum(jnp.sum(loss_rows[:, 0]), "tp")
+    distill_loss = loss_total / (loss_rows.shape[0] * TPS)
+    return (teacher_next[None], distill_loss, grad_local[None], grad_proj)
+
+
 def solution(mesh):
+    fits = mesh.shape["section"] == SECTIONS and mesh.shape["tp"] == TPS
     placed = (
         P("section", "tp", None),
         P("section", None),
@@ -185,7 +865,7 @@
         P("tp", "section"),
     )
     return jax.shard_map(
-        shards,
+        kernel_shards if fits else shards,
         mesh=mesh,
         in_specs=placed,
         out_specs=(P("section", "tp", None), P(), P("section", "tp", None), P("tp", "section")),

time: 370 us -> 198 us (0.54)
  Pallas kernels: 0 us -> 165 us
  waiting for transfers between devices: 112 us -> 0 us
  other arithmetic: 72.4 us -> 5.4 us
  matrix products: 61 us -> 1.28 us
  blocking collectives: 62.8 us -> 14.6 us
  local copies, waits for them, and re-layouts: 42.7 us -> 8.37 us
  between operations: 18 us -> 3.16 us
    pallas_call x0 -> x4, Pallas kernels: none -> 165 us  [the longest x2 56.9 us: scatter(): pl.pallas_call(functools.partial(scatter_kernel, teacher), out_shape=shap...]
    reduce_scatter x2 -> x0, waiting for transfers between devices: 71.4 us -> none  [the longest x1 71.4 us: shards(): lax.psum_scatter(round_bf16(jnp.dot(block, out_local, preferred_element_t...]
    dot_general x5 -> x0, matrix products: 51.4 us -> none  [the longest x1 12.6 us: shards(): lax.dot_general(slope, lax.all_gather(projector, 'tp', axis=0, tiled=True...]
    unnamed x1 -> x0, other arithmetic: 45.2 us -> none
    all_to_all x2 -> x0, blocking collectives: 40.3 us -> none  [the longest x1 21.5 us: shards(): lax.all_to_all(gathered, 'tp', split_axis=2, concat_axis=1, tiled=True)]
    all_gather x4 -> x0, waiting for transfers between devices: 38.8 us -> none  [the longest x1 38.7 us: shards(): block_rows = lax.all_gather(normed, 'tp', axis=0, tiled=True)]
    unnamed x15 -> x7, local copies, waits for them, and re-layouts: 22.9 us -> 7.37 us
    mul x2 -> x0, other arithmetic: 9.05 us -> none  [the longest x1 8.44 us: shards(): target * target]
  transfers between devices with their start and end apart: 6 -> 0, of which waited for: 2 -> 0; matrix products, arithmetic and copies ran while one was open for 28% -> 0% of each run, Pallas kernels for 0% -> 0%
where the time goes in v1:
time: 198 us
  Pallas kernels  165 us (83%)
  blocking collectives  14.6 us (7%)
  local copies, waits for them, and re-layouts  8.37 us (4%)
  other arithmetic  5.4 us (3%)
  between operations  3.16 us (2%)
    pallas_call x2, Pallas kernels, scatter(): pl.pallas_call(functools.partial(scatter_kernel, teacher), out_shape=shap...  56.9 us
    pallas_call x1, Pallas kernels, gradients(): pl.pallas_call(grad_kernel, out_shape=(jax.ShapeDtypeStruct((rows, part *...  56.1 us
    pallas_call x1, Pallas kernels, project(): pl.pallas_call(project_kernel, out_shape=(jax.ShapeDtypeStruct((total, q_...  52.2 us
    psum x1, blocking collectives, kernel_shards(): loss_total = lax.psum(jnp.sum(loss_rows[:, 0]), 'tp')  14.6 us
    unnamed x7, local copies, waits for them, and re-layouts  7.37 us

profile of v1, /device:TPU:0, one launch (start us, length us, event | category | flops | bytes accessed | tf_op | source)
XLA Modules:
  0.0 198.0 jit_solution(11933313367430328077)
XLA Ops:
  1.3 1.3 fusion.2
  2.5 0.1 fusion.10
  2.7 2.0 %fusion.4.normed = bf16[32,8192]{1,0:T(8,128)(2,1)} fusion(f32[8192]{0:T(1024)} %bitcast.64, f32[32]{0:T(128)S(1)} %add_rsqrt_fusion, bf16[1,32,8192]{2,1,0:T(8,128)(2,1)} %param.8), kind=kLoop, calls=%fused_computation.10 | loop fusion | flops 1048576 | bytes 1081472 | tf_op jit(solution)/shard_map/convert_element_type | solution.py:839
  4.7 52.2 %gather_project.1 = (bf16[256,1280]{1,0:T(8,128)(2,1)}, bf16[8,4,32,512]{3,2,1,0:T(8,128)(2,1)}) custom-call(bf16[32,8192]{1,0:T(8,128)(2,1)} %fusion.4.normed, bf16[32,4096]{1,0:T(8,128)(2,1)} %bitcast.63, bf16[8192,1024]{1,0:T(8,128)(2,1)} %bitcast.54, bf16[2,8192,128]{2,1,0:T(8,128)(2,1)} %bitcast.57), custom_call_target="tpu_custom_call" | custom-call | tf_op jit(solution)/shard_map/gather_project/pallas_call | solution.py:377
  57.0 0.0 copy-start.1
  57.0 27.7 %scatter_student.1.student_proj = f32[128,2048]{1,0:T(8,128)} custom-call(bf16[1024,512]{1,0:T(8,128)(2,1)} %bitcast.58, bf16[512,2048]{1,0:T(8,128)(2,1)} %proj_hbm.1), custom_call_target="tpu_custom_call" | custom-call | tf_op jit(solution)/shard_map/scatter_student/pallas_call | solution.py:589
  84.7 0.0 copy-done.1
  84.7 0.5 fusion
  85.1 0.5 fusion.1
  85.7 0.8 convolution_convert_fusion
  86.5 1.0 copy.19.lhs
  87.5 29.2 %scatter_teacher.1 = (bf16[32,8192]{1,0:T(8,128)(2,1)}, bf16[4,32,2048]{2,1,0:T(8,128)(2,1)}) custom-call(bf16[256,1024]{1,0:T(8,128)(2,1)} %copy.19.lhs, bf16[1024,8192]{1,0:T(8,128)(2,1)} %bitcast.55, bf16[32,8192]{1,0:T(8,128)(2,1)} %bitcast.56), custom_call_target="tpu_custom_call" | custom-call | tf_op jit(solution)/shard_map/scatter_teacher/pallas_call | solution.py:589
  116.7 0.0 copy-start
  116.7 56.1 %slope_gradients.1 = (f32[32,4096]{1,0:T(8,128)}, f32[512,2048]{1,0:T(8,128)}, f32[128,128]{1,0:T(8,128)}) custom-call(f32[128,2048]{1,0:T(8,128)} %scatter_student.1.student_proj, bf16[128,2048]{1,0:T(8,128)(2,1)} %bitcast.59, bf16[8,4,32,512]{3,2,1,0:T(8,128)(2,1)} %get-tuple-element.13.feats, bf16[512,2048]{1,0:T(8,128)(2,1)} %proj_hbm.1), custom_call_target="tpu_custom_call" | custom-call | tf_op jit(solution)/shard_map/slope_gradients/pallas_call | solution.py:792
  172.8 1.5 slice_reduce_fusion
  174.3 14.6 %psum.7 = f32[]{:T(128)} all-reduce(f32[]{:T(128)} %slice_reduce_fusion), channel_id=1, replica_groups=mesh['section'=4,'tp'=8] {'tp'}, use_global_device_ids=true, to_apply=%region_4.5 | all-reduce | flops 1 | bytes 8 | tf_op jit(solution)/shard_map/psum | solution.py:850
  189.5 0.0 copy-done
  189.5 0.8 copy.31
  190.3 1.9 copy.32
  192.2 4.7 %copy.33 = f32[512,2048]{1,0:T(8,128)} copy(f32[512,2048]{1,0:T(8,128)} %get-tuple-element.27) | data formatting | bytes 8388608
  (2 shorter events, 0.0 us)
Async XLA Ops:
  57.0 27.7 %copy-start.1 = (bf16[256,1280]{1,0:T(8,128)(2,1)S(1)}, bf16[256,1280]{1,0:T(8,128)(2,1)}, u32[]{:S(2)}) copy-start(bf16[256,1280]{1,0:T(8,128)(2,1)} %get-tuple-element.11) | copy-start | bytes 1966084
  116.7 72.8 %copy-start = (bf16[32,8192]{1,0:T(8,128)(2,1)S(1)}, bf16[32,8192]{1,0:T(8,128)(2,1)}, u32[]{:S(2)}) copy-start(bf16[32,8192]{1,0:T(8,128)(2,1)} %get-tuple-element.12) | copy-start | bytes 1572868

commit v2 on v1

--- a/solution.py
+++ b/solution.py
@@ -199,19 +199,11 @@
     return section, tp, core, x, y, sib, first, second, diag
 
 
-def greet_all(section, tp):
-    barrier = pltpu.get_barrier_semaphore()
-    me = section * TPS + tp
-
-    def one(step, carry):
-        other = (me + step) % (SECTIONS * TPS)
-        pl.semaphore_signal(
-            barrier, inc=1, device_id=(other // TPS, other % TPS), device_id_type=MESH
-        )
-        return carry
-
-    lax.fori_loop(1, SECTIONS * TPS, one, 0)
-    pl.semaphore_wait(barrier, SECTIONS * TPS - 1)
+def greet_lines(section, tp):
+    greet(
+        [(section, (tp + d) % TPS) for d in range(1, TPS)]
+        + [((section + d) % SECTIONS, tp) for d in range(1, SECTIONS)]
+    )
 
 
 def greet(peers):
@@ -265,16 +257,15 @@
 
 
 def project_kernel(
-    normed, student, wq_hbm, wkv_hbm,
+    span, gain, student, wq_hbm, wkv_hbm,
     qkv, feats,
     buf, wq, wkv, acc, acc_k, acc_v,
-    g_send, g_recv, s_send, s_recv, w_sem,
+    g_send, g_recv, s_send, s_recv, z_send, z_recv, w_sem,
 ):
     section, tp, core, x, y, sib, first, second, diag = places()
     chunks, width = buf.shape[0], buf.shape[2]
-    rows = normed.shape[0]
+    rows = span.shape[0]
     part = feats.shape[3]
-    me = section * TPS + tp
 
     def wq_copy(c):
         at = pl.ds(pl.multiple_of(c * width, width), width)
@@ -288,40 +279,59 @@
         wq_copy(c).start()
         wkv_copy(c).start()
         at = pl.ds(pl.multiple_of(c * width, width), width)
-        buf[c, pl.ds(pl.multiple_of(tp * rows, rows), rows)] = normed[:, at]
+        values = span[:, at].astype(F32)
+        return carry + jnp.sum(values * values, axis=1, keepdims=True)
+
+    squares = lax.fori_loop(0, chunks, load, jnp.zeros((rows, 1), F32))
+    inverse = lax.rsqrt(squares / (chunks * width) + NORM_EPS)
+
+    def normalize(c, carry):
+        at = pl.ds(pl.multiple_of(c * width, width), width)
+        values = (span[:, at].astype(F32) * inverse * gain[:, at]).astype(BF16)
+        buf[c, pl.ds(pl.multiple_of(tp * rows, rows), rows)] = values
         return carry
 
-    lax.fori_loop(0, chunks, load, 0)
+    lax.fori_loop(0, chunks, normalize, 0)
     feats[tp, section] = student[:, pl.ds(pl.multiple_of(tp * part, part), part)]
     acc[...] = jnp.zeros_like(acc)
     acc_k[...] = jnp.zeros_like(acc_k)
     acc_v[...] = jnp.zeros_like(acc_v)
-    greet_all(section, tp)
+    greet_lines(section, tp)
     begin, forward, across, arrive, drain = gather_ops(buf, rows, g_send, g_recv)
 
     def s_copy(step):
-        other = (me + step) % (SECTIONS * TPS)
-        to_section, to_tp = other // TPS, other % TPS
-        return pltpu.make_async_remote_copy(
-            src_ref=student.at[:, pl.ds(pl.multiple_of(to_tp * part, part), part)],
+        other = (tp + step) % TPS
+        return pltpu.make_async_remote_copy(
+            src_ref=student.at[:, pl.ds(pl.multiple_of(other * part, part), part)],
             dst_ref=feats.at[tp, section],
             send_sem=s_send.at[step],
             recv_sem=s_recv.at[step],
-            device_id=(to_section, to_tp),
-            device_id_type=MESH,
-        )
+            device_id=(section, other),
+            device_id_type=MESH,
+        )
+
+    def z_copy(d):
+        return pltpu.make_async_remote_copy(
+            src_ref=feats.at[:, section],
+            dst_ref=feats.at[:, section],
+            send_sem=z_send.at[d],
+            recv_sem=z_recv.at[d],
+            device_id=((section + d) % SECTIONS, tp),
+            device_id_type=MESH,
+        )
+
+    for d in range(1, TPS):
+        s_copy(d).start()
 
     def start_gather(c, carry):
         begin(c)
         return carry
 
     lax.fori_loop(0, chunks, start_gather, 0)
-
-    def start_student(step, carry):
-        s_copy(step).start()
-        return carry
-
-    lax.fori_loop(1, SECTIONS * TPS, start_student, 0)
+    for d in range(1, TPS):
+        s_copy(d).wait()
+    for d in (2, 1, 3):
+        z_copy(d).start()
 
     def step(i, carry):
         @pl.when(i < chunks)
@@ -359,15 +369,12 @@
 
     lax.fori_loop(0, chunks, finish, 0)
 
-    def finish_student(step, carry):
-        s_copy(step).wait()
-        return carry
-
-    lax.fori_loop(1, SECTIONS * TPS, finish_student, 0)
-
-
-def project(normed, student, wq, wkv):
-    rows, depth = normed.shape
+    for d in (1, 2, 3):
+        z_copy(d).wait()
+
+
+def project(span, gain, student, wq, wkv):
+    rows, depth = span.shape
     total = rows * TPS
     q_cols, k_cols = wq.shape[1], wkv.shape[2]
     chunks = 8
@@ -380,7 +387,7 @@
             jax.ShapeDtypeStruct((total, q_cols + 2 * k_cols), BF16),
             jax.ShapeDtypeStruct((TPS, SECTIONS, rows, part), BF16),
         ),
-        in_specs=[vmem, vmem, hbm, hbm],
+        in_specs=[vmem, vmem, vmem, hbm, hbm],
         out_specs=(vmem, vmem),
         scratch_shapes=[
             pltpu.VMEM((chunks, total, depth // chunks), BF16),
@@ -391,15 +398,17 @@
             pltpu.VMEM((total, k_cols), F32),
             pltpu.SemaphoreType.DMA((7, chunks)),
             pltpu.SemaphoreType.DMA((7, chunks)),
-            pltpu.SemaphoreType.DMA((SECTIONS * TPS,)),
-            pltpu.SemaphoreType.DMA((SECTIONS * TPS,)),
+            pltpu.SemaphoreType.DMA((TPS,)),
+            pltpu.SemaphoreType.DMA((TPS,)),
+            pltpu.SemaphoreType.DMA((SECTIONS,)),
+            pltpu.SemaphoreType.DMA((SECTIONS,)),
             pltpu.SemaphoreType.DMA((2, chunks)),
         ],
         compiler_params=pltpu.CompilerParams(
             collective_id=0, has_side_effects=True, vmem_limit_bytes=VMEM_LIMIT
         ),
         name="gather_project",
-    )(normed, student, wq, wkv)
+    )(span, gain, student, wq, wkv)
 
 
 def scatter_kernel(
@@ -602,11 +611,10 @@
 def grad_kernel(
     student_proj, target, feats, proj_hbm,
     grad_s, grad_p, loss,
-    proj, buf, gs, gs_out, landed, sums, sums_in, flat, back,
-    g_send, g_recv, a_send, a_recv, z_send, z_recv, w_sem,
+    proj, buf, gs, gs_out, landed, summed, pieces, sums_in, lost, flat, back,
+    g_send, g_recv, a_send, a_recv, l_send, l_recv, z_send, z_recv, p_send, p_recv, w_sem,
 ):
     section, tp, core, x, y, sib, first, second, diag = places()
-    me = section * TPS + tp
     chunks, _, width = buf.shape
     rows = grad_s.shape[0]
     parts = chunks // SECTIONS
@@ -620,14 +628,14 @@
     goal_sq = jnp.sum(goal * goal, axis=1, keepdims=True)
     table = jnp.where(lane == 0, inner, jnp.where(lane == 1, own_sq, goal_sq))
     flat[...] = table.T
-    sums[...] = flat[:8]
-    greet_all(section, tp)
+    sums_in[section] = flat[:8]
+    greet_lines(section, tp)
 
     def a_copy(d):
         other = (section + d) % SECTIONS
         return pltpu.make_async_remote_copy(
-            src_ref=sums,
-            dst_ref=sums_in.at[d - 1],
+            src_ref=sums_in.at[section],
+            dst_ref=sums_in.at[section],
             send_sem=a_send.at[d - 1],
             recv_sem=a_recv.at[d - 1],
             device_id=(other, tp),
@@ -639,20 +647,35 @@
     grad_p[...] = jnp.zeros_like(grad_p)
     for d in (1, 2, 3):
         a_copy(d).wait()
-    flat[:8] = sums[...] + sums_in[0] + sums_in[1] + sums_in[2]
+    flat[:8] = sums_in[0] + sums_in[1] + sums_in[2] + sums_in[3]
     back[...] = flat[...].T
     table = back[...]
     inner, own_sq, goal_sq = table[:, 0:1], table[:, 1:2], table[:, 2:3]
     inv_own = lax.rsqrt(own_sq + COS_EPS)
     inv_goal = lax.rsqrt(goal_sq + COS_EPS)
     cosine = inner * inv_own * inv_goal
-    loss[...] = jnp.broadcast_to(1.0 - cosine, loss.shape)
+    distance = jnp.sum(jnp.broadcast_to(1.0 - cosine, back.shape), axis=0, keepdims=True)
+    lost[tp] = jnp.broadcast_to(distance, loss.shape)
+
+    def l_copy(d):
+        return pltpu.make_async_remote_copy(
+            src_ref=lost.at[tp],
+            dst_ref=lost.at[tp],
+            send_sem=l_send.at[d],
+            recv_sem=l_recv.at[d],
+            device_id=(section, (tp + d) % TPS),
+            device_id_type=MESH,
+        )
+
     up = LOSS_WEIGHT * (inner * inv_goal * inv_own * inv_own * inv_own)
     down = LOSS_WEIGHT * (inv_own * inv_goal)
     back[...] = jnp.where(lane == 0, up, down)
 
     def block_of(i):
-        return (section + 2 + i // parts) % SECTIONS, i % parts
+        turn = i // parts
+        late = turn // 2
+        apart = (1 - late) * (2 + turn) + late * (3 - turn)
+        return (section + apart) % SECTIONS, i % parts
 
     def at_tp(index):
         return pl.ds(pl.multiple_of(index * rows, rows), rows)
@@ -673,27 +696,38 @@
         return carry
 
     lax.fori_loop(0, chunks, make, 0)
+    for d in range(1, TPS):
+        l_copy(d).start()
     load.wait()
 
-    def z_copy(s, step):
-        other = (tp + step) % TPS
-        return pltpu.make_async_remote_copy(
-            src_ref=gs_out.at[s, at_tp(other)],
-            dst_ref=landed.at[section, tp],
-            send_sem=z_send.at[s, step],
-            recv_sem=z_recv.at[section, tp],
-            device_id=(s, other),
-            device_id_type=MESH,
-        )
-
-    def z_land(s, t):
-        place = landed.at[s, t]
-        return pltpu.make_async_remote_copy(
-            src_ref=place,
-            dst_ref=place,
-            send_sem=z_send.at[0, 0],
-            recv_sem=z_recv.at[s, t],
-            device_id=(section, tp),
+    def z_copy(s):
+        return pltpu.make_async_remote_copy(
+            src_ref=gs_out.at[s],
+            dst_ref=landed.at[section],
+            send_sem=z_send.at[s],
+            recv_sem=z_recv.at[section],
+            device_id=(s, tp),
+            device_id_type=MESH,
+        )
+
+    def z_land(s):
+        return pltpu.make_async_remote_copy(
+            src_ref=gs_out.at[s],
+            dst_ref=landed.at[s],
+            send_sem=z_send.at[s],
+            recv_sem=z_recv.at[s],
+            device_id=(s, tp),
+            device_id_type=MESH,
+        )
+
+    def p_copy(d):
+        other = (tp + d) % TPS
+        return pltpu.make_async_remote_copy(
+            src_ref=summed.at[at_tp(other)],
+            dst_ref=pieces.at[tp],
+            send_sem=p_send.at[d],
+            recv_sem=p_recv.at[d],
+            device_id=(section, other),
             device_id_type=MESH,
         )
 
@@ -719,18 +753,13 @@
         def _():
             gs_out[s] = gs[...].astype(BF16)
 
-            def push(step, carry):
-                @pl.when((s != section) | (step > 0))
-                def _():
-                    z_copy(s, step).start()
-
-                return carry
-
-            lax.fori_loop(0, TPS, push, 0)
+            @pl.when(s != section)
+            def _():
+                z_copy(s).start()
 
             @pl.when(s == section)
             def _():
-                landed[section, tp] = gs_out[section, at_tp(tp)]
+                landed[section] = gs_out[section]
 
         tokens = feats[:, s].reshape(TPS * rows, feats.shape[3])
         grad_p[:, cols] += lax.dot_general(tokens, slopes, first_dims, preferred_element_type=F32)
@@ -751,33 +780,35 @@
         return carry
 
     lax.fori_loop(0, chunks + 2, step, 0)
+
+    for d in range(1, SECTIONS):
+        z_land((section + d) % SECTIONS).wait_recv()
+    total = landed[0].astype(F32)
+    for s in range(1, SECTIONS):
+        total += landed[s].astype(F32)
+    summed[...] = total.astype(BF16)
+    for d in range(1, TPS):
+        p_copy(d).start()
+    pieces[tp] = summed[at_tp(tp)]
+    for d in range(1, TPS):
+        l_copy(d).wait()
+    total = lost[0]
+    for t in range(1, TPS):
+        total += lost[t]
+    loss[...] = total / (SECTIONS * rows * TPS)
 
     def finish(i, carry):
         drain(i)
         return carry
 
     lax.fori_loop(0, chunks, finish, 0)
-
-    def finish_z(i, carry):
-        s, step = i // TPS, i % TPS
-
-        @pl.when((s != section) | (step > 0))
-        def _():
-            z_copy(s, step).wait_send()
-
-        @pl.when((s != section) | (step != tp))
-        def _():
-            z_land(s, step).wait_recv()
-
-        return carry
-
-    lax.fori_loop(0, SECTIONS * TPS, finish_z, 0)
-    part = landed.shape[3]
+    for d in range(1, SECTIONS):
+        z_copy((section + d) % SECTIONS).wait_send()
+    for d in range(1, TPS):
+        p_copy(d).wait()
+    part = pieces.shape[2]
     for t in range(TPS):
-        total = landed[0, t].astype(F32)
-        for s in range(1, SECTIONS):
-            total += landed[s, t].astype(F32)
-        grad_s[:, t * part : (t + 1) * part] = total
+        grad_s[:, t * part : (t + 1) * part] = pieces[t].astype(F32)
 
 
 def gradients(student_proj, target, feats, proj):
@@ -794,7 +825,7 @@
         out_shape=(
             jax.ShapeDtypeStruct((rows, part * TPS), F32),
             jax.ShapeDtypeStruct((part, cols), F32),
-            jax.ShapeDtypeStruct((tokens, 128), F32),
+            jax.ShapeDtypeStruct((8, 128), F32),
         ),
         in_specs=[vmem, vmem, vmem, hbm],
         out_specs=(vmem, vmem, vmem),
@@ -803,17 +834,23 @@
             pltpu.VMEM((chunks, TPS * rows, width), BF16),
             pltpu.VMEM((TPS * rows, part), F32),
             pltpu.VMEM((SECTIONS, TPS * rows, part), BF16),
-            pltpu.VMEM((SECTIONS, TPS, rows, part), BF16),
-            pltpu.VMEM((8, tokens), F32),
-            pltpu.VMEM((SECTIONS - 1, 8, tokens), F32),
+            pltpu.VMEM((SECTIONS, TPS * rows, part), BF16),
+            pltpu.VMEM((TPS * rows, part), BF16),
+            pltpu.VMEM((TPS, rows, part), BF16),
+            pltpu.VMEM((SECTIONS, 8, tokens), F32),
+            pltpu.VMEM((TPS, 8, 128), F32),
             pltpu.VMEM((128, tokens), F32),
             pltpu.VMEM((tokens, 128), F32),
             dma((7, chunks)),
             dma((7, chunks)),
             dma((SECTIONS - 1,)),
             dma((SECTIONS - 1,)),
-            dma((SECTIONS, TPS)),
-            dma((SECTIONS, TPS)),
+            dma((TPS,)),
+            dma((TPS,)),
+            dma((SECTIONS,)),
+            dma((SECTIONS,)),
+            dma((TPS,)),
+            dma((TPS,)),
             dma((1,)),
         ],
         compiler_params=pltpu.CompilerParams(
@@ -834,21 +871,19 @@
     projector,
 ):
     span_rows = teacher_rows[0]
-    rows_float = span_rows.astype(F32)
-    mean_square = jnp.mean(rows_float * rows_float, axis=1, keepdims=True)
-    normed = (rows_float * lax.rsqrt(mean_square + NORM_EPS) * norm_gain[0][None, :]).astype(BF16)
-    qkv, feats = project(normed, student_rows[0], query_weight[0], keys_values[0])
+    qkv, feats = project(
+        span_rows, norm_gain, student_rows[0], query_weight[0], keys_values[0]
+    )
     q_cols = query_weight.shape[2]
     student_proj = scatter(feats.reshape(-1, feats.shape[3]), projector)
     mixed = attend(
         qkv[:, :q_cols], qkv[:, q_cols : q_cols + HD], qkv[:, q_cols + HD :], doc_start[0]
     )
     teacher_next, target = scatter(mixed, output_weight[0], span_rows)
-    grad_local, grad_proj, loss_rows = gradients(
+    grad_local, grad_proj, loss = gradients(
         student_proj, target.reshape(-1, target.shape[2]), feats, projector
     )
-    loss_total = lax.psum(jnp.sum(loss_rows[:, 0]), "tp")
-    distill_loss = loss_total / (loss_rows.shape[0] * TPS)
+    distill_loss = loss[0, 0]
     return (teacher_next[None], distill_loss, grad_local[None], grad_proj)
 
 

time: 198 us -> 170 us (0.86)
  blocking collectives: 14.6 us -> 0 us
  Pallas kernels: 165 us -> 156 us
  other arithmetic: 5.4 us -> 0.63 us
    psum x1 -> x0, blocking collectives: 14.6 us -> none  [kernel_shards(): loss_total = lax.psum(jnp.sum(loss_rows[:, 0]), 'tp')]
    pallas_call x1, Pallas kernels: 52.2 us -> 42.2 us  [project(): pl.pallas_call(project_kernel, out_shape=(jax.ShapeDtypeStruct((total, q_...]
    reduce_sum x2 -> x0, other arithmetic: 2.71 us -> none  [the longest x1 1.46 us: kernel_shards(): loss_total = lax.psum(jnp.sum(loss_rows[:, 0]), 'tp')]
    convert_element_type x1 -> x0, other arithmetic: 2.04 us -> none  [kernel_shards(): (rows_float * lax.rsqrt(mean_square + NORM_EPS) * norm_gain[0][None, :])....]
where the time goes in v2:
time: 170 us; the launch traced here: 168 us
  Pallas kernels  156 us (92%)
  local copies, waits for them, and re-layouts  9.55 us (6%)
    pallas_call x2, Pallas kernels, scatter(): pl.pallas_call(functools.partial(scatter_kernel, teacher), out_shape=shap...  57.6 us
    pallas_call x1, Pallas kernels, gradients(): pl.pallas_call(grad_kernel, out_shape=(jax.ShapeDtypeStruct((rows, part *...  55.8 us
    pallas_call x1, Pallas kernels, project(): pl.pallas_call(project_kernel, out_shape=(jax.ShapeDtypeStruct((total, q_...  42.2 us
    unnamed x7, local copies, waits for them, and re-layouts  7.37 us

profile of v2, /device:TPU:0, one launch (start us, length us, event | category | flops | bytes accessed | tf_op | source)
XLA Modules:
  0.0 168.5 jit_solution(1907155457612784274)
XLA Ops:
  1.3 0.1 fusion.7
  1.4 42.2 %gather_project.1 = (bf16[256,1280]{1,0:T(8,128)(2,1)}, bf16[8,4,32,512]{3,2,1,0:T(8,128)(2,1)}) custom-call(bf16[32,8192]{1,0:T(8,128)(2,1)} %bitcast.56, f32[1,8192]{1,0:T(1,128)} %gain.1, bf16[32,4096]{1,0:T(8,128)(2,1)} %bitcast.62, bf16[8192,1024]{1,0:T(8,128)(2,1)} %bitcast.52, bf16[2,8192,128]{2,1,0:T(8,128)(2,1)} %bitcast.54), custom_call_target="tpu_custom_call" | custom-call | tf_op jit(solution)/shard_map/gather_project/pallas_call | solution.py:384
  43.6 0.0 copy-start.1
  43.6 27.7 %scatter_student.1.student_proj = f32[128,2048]{1,0:T(8,128)} custom-call(bf16[1024,512]{1,0:T(8,128)(2,1)} %bitcast.55, bf16[512,2048]{1,0:T(8,128)(2,1)} %proj_hbm.1), custom_call_target="tpu_custom_call" | custom-call | tf_op jit(solution)/shard_map/scatter_student/pallas_call | solution.py:598
  71.3 0.0 copy-done.1
  71.3 0.5 fusion
  71.8 0.5 fusion.1
  72.3 0.8 convolution_convert_fusion
  73.1 1.0 copy.19.lhs
  74.2 29.9 %scatter_teacher.1 = (bf16[32,8192]{1,0:T(8,128)(2,1)}, bf16[4,32,2048]{2,1,0:T(8,128)(2,1)}) custom-call(bf16[256,1024]{1,0:T(8,128)(2,1)} %copy.19.lhs, bf16[1024,8192]{1,0:T(8,128)(2,1)} %bitcast.53, bf16[32,8192]{1,0:T(8,128)(2,1)} %bitcast.57), custom_call_target="tpu_custom_call" | custom-call | tf_op jit(solution)/shard_map/scatter_teacher/pallas_call | solution.py:598
  104.1 0.0 copy-start
  104.1 55.8 %slope_gradients.1 = (f32[32,4096]{1,0:T(8,128)}, f32[512,2048]{1,0:T(8,128)}, f32[8,128]{1,0:T(8,128)}) custom-call(f32[128,2048]{1,0:T(8,128)} %scatter_student.1.student_proj, bf16[128,2048]{1,0:T(8,128)(2,1)} %bitcast.58, bf16[8,4,32,512]{3,2,1,0:T(8,128)(2,1)} %get-tuple-element.13.feats, bf16[512,2048]{1,0:T(8,128)(2,1)} %proj_hbm.1), custom_call_target="tpu_custom_call" | custom-call | tf_op jit(solution)/shard_map/slope_gradients/pallas_call | solution.py:823
  159.9 1.2 slice.15
  161.1 0.0 copy-done
  161.1 0.8 copy.31
  161.9 1.9 %copy.32 = f32[1,32,4096]{2,1,0:T(8,128)} copy(f32[1,32,4096]{2,1,0:T(8,128)} %bitcast.60) | data formatting | bytes 1048576
  163.8 4.7 %copy.33 = f32[512,2048]{1,0:T(8,128)} copy(f32[512,2048]{1,0:T(8,128)} %get-tuple-element.27) | data formatting | bytes 8388608
  (1 shorter events, 0.0 us)
Async XLA Ops:
  43.6 27.7 %copy-start.1 = (bf16[256,1280]{1,0:T(8,128)(2,1)S(1)}, bf16[256,1280]{1,0:T(8,128)(2,1)}, u32[]{:S(2)}) copy-start(bf16[256,1280]{1,0:T(8,128)(2,1)} %get-tuple-element.11) | copy-start | bytes 1966084
  104.1 57.0 %copy-start = (bf16[32,8192]{1,0:T(8,128)(2,1)S(1)}, bf16[32,8192]{1,0:T(8,128)(2,1)}, u32[]{:S(2)}) copy-start(bf16[32,8192]{1,0:T(8,128)(2,1)} %get-tuple-element.12) | copy-start | bytes 1572868

commit v3 on v2

--- a/solution.py
+++ b/solution.py
@@ -258,14 +258,14 @@
 
 def project_kernel(
     span, gain, student, wq_hbm, wkv_hbm,
-    qkv, feats,
+    qkv, plane,
     buf, wq, wkv, acc, acc_k, acc_v,
-    g_send, g_recv, s_send, s_recv, z_send, z_recv, w_sem,
+    g_send, g_recv, s_send, s_recv, w_sem,
 ):
     section, tp, core, x, y, sib, first, second, diag = places()
     chunks, width = buf.shape[0], buf.shape[2]
     rows = span.shape[0]
-    part = feats.shape[3]
+    part = plane.shape[2]
 
     def wq_copy(c):
         at = pl.ds(pl.multiple_of(c * width, width), width)
@@ -292,34 +292,24 @@
         return carry
 
     lax.fori_loop(0, chunks, normalize, 0)
-    feats[tp, section] = student[:, pl.ds(pl.multiple_of(tp * part, part), part)]
+    plane[tp] = student[:, pl.ds(pl.multiple_of(tp * part, part), part)]
     acc[...] = jnp.zeros_like(acc)
     acc_k[...] = jnp.zeros_like(acc_k)
     acc_v[...] = jnp.zeros_like(acc_v)
-    greet_lines(section, tp)
+    greet([(section, (tp + d) % TPS) for d in range(1, TPS)])
     begin, forward, across, arrive, drain = gather_ops(buf, rows, g_send, g_recv)
 
     def s_copy(step):
         other = (tp + step) % TPS
         return pltpu.make_async_remote_copy(
             src_ref=student.at[:, pl.ds(pl.multiple_of(other * part, part), part)],
-            dst_ref=feats.at[tp, section],
+            dst_ref=plane.at[tp],
             send_sem=s_send.at[step],
             recv_sem=s_recv.at[step],
             device_id=(section, other),
             device_id_type=MESH,
         )
 
-    def z_copy(d):
-        return pltpu.make_async_remote_copy(
-            src_ref=feats.at[:, section],
-            dst_ref=feats.at[:, section],
-            send_sem=z_send.at[d],
-            recv_sem=z_recv.at[d],
-            device_id=((section + d) % SECTIONS, tp),
-            device_id_type=MESH,
-        )
-
     for d in range(1, TPS):
         s_copy(d).start()
 
@@ -328,10 +318,6 @@
         return carry
 
     lax.fori_loop(0, chunks, start_gather, 0)
-    for d in range(1, TPS):
-        s_copy(d).wait()
-    for d in (2, 1, 3):
-        z_copy(d).start()
 
     def step(i, carry):
         @pl.when(i < chunks)
@@ -369,8 +355,8 @@
 
     lax.fori_loop(0, chunks, finish, 0)
 
-    for d in (1, 2, 3):
-        z_copy(d).wait()
+    for d in range(1, TPS):
+        s_copy(d).wait()
 
 
 def project(span, gain, student, wq, wkv):
@@ -385,7 +371,7 @@
         project_kernel,
         out_shape=(
             jax.ShapeDtypeStruct((total, q_cols + 2 * k_cols), BF16),
-            jax.ShapeDtypeStruct((TPS, SECTIONS, rows, part), BF16),
+            jax.ShapeDtypeStruct((TPS, rows, part), BF16),
         ),
         in_specs=[vmem, vmem, vmem, hbm, hbm],
         out_specs=(vmem, vmem),
@@ -400,8 +386,6 @@
             pltpu.SemaphoreType.DMA((7, chunks)),
             pltpu.SemaphoreType.DMA((TPS,)),
             pltpu.SemaphoreType.DMA((TPS,)),
-            pltpu.SemaphoreType.DMA((SECTIONS,)),
-            pltpu.SemaphoreType.DMA((SECTIONS,)),
             pltpu.SemaphoreType.DMA((2, chunks)),
         ],
         compiler_params=pltpu.CompilerParams(
@@ -415,26 +399,19 @@
     teacher, lhs, rhs_hbm, *refs,
 ):
     if teacher:
-        resid, out, shared = refs[:3]
+        resid, moved, out, shared = refs[:4]
+        refs = refs[4:]
+    else:
+        moved, out, shared = refs[:3]
         refs = refs[3:]
-    else:
-        out = refs[0]
-        refs = refs[1:]
-    rhs, part, sib_buf, pair, got1, half, got2, sends, recvs, w_sem = refs[:10]
-    if teacher:
-        z_send, z_recv = refs[10:]
+    rhs, part, sib_buf, pair, got1, half, got2, sends, recvs, w_sem, z_send, z_recv = refs
     section, tp, core, x, y, sib, first, second, diag = places()
     chunks, _, m, width = part.shape
     f_mine = (1 - core) * x + core * y
     g_mine = core * x + (1 - core) * y
 
-    def column(i):
-        if teacher:
-            return (i % SECTIONS) * (chunks // SECTIONS) + i // SECTIONS
-        return i
-
     def columns(i):
-        return pl.ds(pl.multiple_of(column(i) * width, width), width)
+        return pl.ds(pl.multiple_of(i * width, width), width)
 
     def w_copy(i):
         return pltpu.make_async_copy(rhs_hbm.at[:, columns(i)], rhs.at[i], w_sem.at[i])
@@ -445,9 +422,32 @@
 
     lax.fori_loop(0, chunks, load, 0)
     peers = [(section, sib), (section, first), (section, second)]
+    peers += [((section + d) % SECTIONS, tp) for d in range(1, SECTIONS)]
     if teacher:
-        peers += [((section + d) % SECTIONS, tp) for d in range(1, SECTIONS)]
+        shared[:, section] = moved[...]
+    else:
+        span = shared.shape[2]
+        shared[section] = moved[:, pl.ds(pl.multiple_of(section * span, span), span)]
     greet(peers)
+
+    def z_copy(d):
+        other = (section + d) % SECTIONS
+        if teacher:
+            source, landing = moved, shared.at[:, section]
+        else:
+            source = moved.at[:, pl.ds(pl.multiple_of(other * span, span), span)]
+            landing = shared.at[section]
+        return pltpu.make_async_remote_copy(
+            src_ref=source,
+            dst_ref=landing,
+            send_sem=z_send.at[d],
+            recv_sem=z_recv.at[d],
+            device_id=(other, tp),
+            device_id_type=MESH,
+        )
+
+    for d in (2, 1, 3):
+        z_copy(d).start()
 
     def remote(kind, i, source, landing, target):
         return pltpu.make_async_remote_copy(
@@ -468,27 +468,6 @@
     def to_second(i):
         return remote(2, i, half.at[i, 1 - g_mine], got2.at[i], second)
 
-    def to_z(i, d):
-        return pltpu.make_async_remote_copy(
-            src_ref=out.at[:, columns(i)],
-            dst_ref=shared.at[section, :, pl.ds(pl.multiple_of((i // SECTIONS) * width, width), width)],
-            send_sem=z_send.at[i],
-            recv_sem=z_recv.at[section, i // SECTIONS],
-            device_id=(i % SECTIONS, tp),
-            device_id_type=MESH,
-        )
-
-    def from_z(other, h):
-        place = shared.at[other, :, pl.ds(pl.multiple_of(h * width, width), width)]
-        return pltpu.make_async_remote_copy(
-            src_ref=place,
-            dst_ref=place,
-            send_sem=z_send.at[0],
-            recv_sem=z_recv.at[other, h],
-            device_id=(other, tp),
-            device_id_type=MESH,
-        )
-
     def stage_a(i):
         w_copy(i).wait()
         block = jnp.dot(lhs[...], rhs[i], preferred_element_type=F32).astype(BF16)
@@ -518,17 +497,7 @@
         if not teacher:
             out[:, columns(i)] = total
             return
-        value = (resid[:, columns(i)].astype(F32) + total).astype(BF16)
-        out[:, columns(i)] = value
-
-        @pl.when(i % SECTIONS == section)
-        def _():
-            at = pl.ds(pl.multiple_of((i // SECTIONS) * width, width), width)
-            shared[section, :, at] = value
-
-        @pl.when(i % SECTIONS != section)
-        def _():
-            to_z(i, 0).start()
+        out[:, columns(i)] = (resid[:, columns(i)].astype(F32) + total).astype(BF16)
 
     ends = (0, 1, 3, 5)
 
@@ -547,22 +516,14 @@
         to_sib(i).wait_send()
         to_first(i).wait_send()
         to_second(i).wait_send()
-        if teacher:
-
-            @pl.when(i % SECTIONS != section)
-            def _():
-                to_z(i, 0).wait_send()
-
-            @pl.when(i % SECTIONS != section)
-            def _():
-                from_z(i % SECTIONS, i // SECTIONS).wait_recv()
-
         return carry
 
     lax.fori_loop(0, chunks, finish, 0)
-
-
-def scatter(lhs, rhs, resid=None):
+    for d in (1, 2, 3):
+        z_copy(d).wait()
+
+
+def scatter(lhs, rhs, moved, resid=None):
     teacher = resid is not None
     depth, cols = rhs.shape
     m = lhs.shape[0] // TPS
@@ -581,20 +542,21 @@
         pltpu.SemaphoreType.DMA((3, chunks)),
         pltpu.SemaphoreType.DMA((3, chunks)),
         pltpu.SemaphoreType.DMA((chunks,)),
+        pltpu.SemaphoreType.DMA((SECTIONS,)),
+        pltpu.SemaphoreType.DMA((SECTIONS,)),
     ]
     if teacher:
-        scratch += [
-            pltpu.SemaphoreType.DMA((chunks,)),
-            pltpu.SemaphoreType.DMA((SECTIONS, chunks // SECTIONS)),
-        ]
         shape = (
             jax.ShapeDtypeStruct((m, cols), BF16),
-            jax.ShapeDtypeStruct((SECTIONS, m, cols // SECTIONS), BF16),
-        )
-        operands = (lhs, rhs, resid)
+            jax.ShapeDtypeStruct((TPS, SECTIONS) + moved.shape[1:], BF16),
+        )
+        operands = (lhs, rhs, resid, moved)
     else:
-        shape = jax.ShapeDtypeStruct((m, cols), F32)
-        operands = (lhs, rhs)
+        shape = (
+            jax.ShapeDtypeStruct((m, cols), F32),
+            jax.ShapeDtypeStruct((SECTIONS, moved.shape[0], cols), BF16),
+        )
+        operands = (lhs, rhs, moved)
     return pl.pallas_call(
         functools.partial(scatter_kernel, teacher),
         out_shape=shape,
@@ -871,15 +833,15 @@
     projector,
 ):
     span_rows = teacher_rows[0]
-    qkv, feats = project(
+    qkv, plane = project(
         span_rows, norm_gain, student_rows[0], query_weight[0], keys_values[0]
     )
     q_cols = query_weight.shape[2]
-    student_proj = scatter(feats.reshape(-1, feats.shape[3]), projector)
     mixed = attend(
         qkv[:, :q_cols], qkv[:, q_cols : q_cols + HD], qkv[:, q_cols + HD :], doc_start[0]
     )
-    teacher_next, target = scatter(mixed, output_weight[0], span_rows)
+    teacher_next, feats = scatter(mixed, output_weight[0], plane, span_rows)
+    student_proj, target = scatter(feats.reshape(-1, feats.shape[3]), projector, teacher_next)
     grad_local, grad_proj, loss = gradients(
         student_proj, target.reshape(-1, target.shape[2]), feats, projector
     )

time: 170 us -> 167 us (0.982)
  Pallas kernels: 156 us -> 151 us
  matrix products: 1.28 us -> 3.2 us
    pallas_call x1, Pallas kernels: 55.8 us -> 52.3 us  [gradients(): pl.pallas_call(grad_kernel, out_shape=(jax.ShapeDtypeStruct((rows, part *...]
    unnamed x7 -> x5, local copies, waits for them, and re-layouts: 7.37 us -> 7.36 us
where the time goes in v3:
time: 167 us; the launch traced here: 166 us
  Pallas kernels  151 us (90%)
  local copies, waits for them, and re-layouts  9.55 us (6%)
  matrix products  3.2 us (2%)
    pallas_call x2, Pallas kernels, scatter(): pl.pallas_call(functools.partial(scatter_kernel, teacher), out_shape=shap...  58 us
    pallas_call x1, Pallas kernels, gradients(): pl.pallas_call(grad_kernel, out_shape=(jax.ShapeDtypeStruct((rows, part *...  52.3 us
    pallas_call x1, Pallas kernels, project(): pl.pallas_call(project_kernel, out_shape=(jax.ShapeDtypeStruct((total, q_...  40.7 us
    unnamed x5, local copies, waits for them, and re-layouts  7.36 us

profile of v3, /device:TPU:0, one launch (start us, length us, event | category | flops | bytes accessed | tf_op | source)
XLA Modules:
  0.0 165.7 jit_solution(6068748786403636031)
XLA Ops:
  1.3 0.1 fusion.7
  1.4 40.7 %gather_project.1 = (bf16[256,1280]{1,0:T(8,128)(2,1)}, bf16[8,32,512]{2,1,0:T(8,128)(2,1)}) custom-call(bf16[32,8192]{1,0:T(8,128)(2,1)} %bitcast.56, f32[1,8192]{1,0:T(1,128)} %gain.1, bf16[32,4096]{1,0:T(8,128)(2,1)} %bitcast.62, bf16[8192,1024]{1,0:T(8,128)(2,1)} %bitcast.52, bf16[2,8192,128]{2,1,0:T(8,128)(2,1)} %bitcast.55), custom_call_target="tpu_custom_call" | custom-call | tf_op jit(solution)/shard_map/gather_project/pallas_call | solution.py:370
  42.1 1.6 fusion
  43.7 0.5 fusion.1
  44.2 1.6 convolution_convert_fusion
  45.8 1.0 copy.19.lhs
  46.8 30.3 %scatter_teacher.1 = (bf16[32,8192]{1,0:T(8,128)(2,1)}, bf16[8,4,32,512]{3,2,1,0:T(8,128)(2,1)}) custom-call(bf16[256,1024]{1,0:T(8,128)(2,1)} %copy.19.lhs, bf16[1024,8192]{1,0:T(8,128)(2,1)} %bitcast.53, bf16[32,8192]{1,0:T(8,128)(2,1)} %bitcast.57, bf16[8,32,512]{2,1,0:T(8,128)(2,1)} %get-tuple-element.14.refs_1_), custom_call_target="tpu_custom_call" | custom-call | tf_op jit(solution)/shard_map/scatter_teacher/pallas_call | solution.py:560
  77.2 27.7 %scatter_student.1 = (f32[128,2048]{1,0:T(8,128)}, bf16[4,32,2048]{2,1,0:T(8,128)(2,1)}) custom-call(bf16[1024,512]{1,0:T(8,128)(2,1)} %bitcast.54, bf16[512,2048]{1,0:T(8,128)(2,1)} %proj_hbm.1, bf16[32,8192]{1,0:T(8,128)(2,1)} %get-tuple-element.15.refs_0_), custom_call_target="tpu_custom_call" | custom-call | tf_op jit(solution)/shard_map/scatter_student/pallas_call | solution.py:560
  104.9 0.0 copy-start
  104.9 52.3 %slope_gradients.1 = (f32[32,4096]{1,0:T(8,128)}, f32[512,2048]{1,0:T(8,128)}, f32[8,128]{1,0:T(8,128)}) custom-call(f32[128,2048]{1,0:T(8,128)} %get-tuple-element.17.student_proj, bf16[128,2048]{1,0:T(8,128)(2,1)} %bitcast.59, bf16[8,4,32,512]{3,2,1,0:T(8,128)(2,1)} %get-tuple-element.16.feats, bf16[512,2048]{1,0:T(8,128)(2,1)} %proj_hbm.1), custom_call_target="tpu_custom_call" | custom-call | tf_op jit(solution)/shard_map/slope_gradients/pallas_call | solution.py:785
  157.1 1.2 slice.15
  158.3 0.0 copy-done
  158.3 0.8 copy.31
  159.1 1.9 %copy.32 = f32[1,32,4096]{2,1,0:T(8,128)} copy(f32[1,32,4096]{2,1,0:T(8,128)} %bitcast.60) | data formatting | bytes 1048576
  161.0 4.7 %copy.33 = f32[512,2048]{1,0:T(8,128)} copy(f32[512,2048]{1,0:T(8,128)} %get-tuple-element.31) | data formatting | bytes 8388608
  (1 shorter events, 0.0 us)
Async XLA Ops:
  104.9 53.5 %copy-start = (bf16[32,8192]{1,0:T(8,128)(2,1)S(1)}, bf16[32,8192]{1,0:T(8,128)(2,1)}, u32[]{:S(2)}) copy-start(bf16[32,8192]{1,0:T(8,128)(2,1)} %get-tuple-element.15.refs_0_) | copy-start | bytes 1572868
